TPU v7x, 32 devices: a whole 2x2x4 slice. The times are simulated.
32 devices in a mesh: narrow: 4 (over z), wide: 8 (over y, x, core).
Axes of the slice: x: 2, y: 2, z: 4, core: 2. Of those that a mesh axis runs over, the one named last changes fastest.
Arguments:
- layer_in: bfloat16 [16384, 1024], P(('narrow', 'wide')), may hold values from -30 to 30
- first_values: bfloat16 [16384, 1024], P(('narrow', 'wide')), may hold values from -6 to 6
- out_grad: bfloat16 [16384, 1024], P(('narrow', 'wide')), may hold values from -6 to 6
- seq_group: int32 [32], P(('narrow', 'wide')), may hold values from 0 to 1
- short_split: int32 [32], P(('narrow', 'wide')), may hold values from 128 to 384
- attn_gain: bfloat16 [1024], P(('narrow', 'wide')), may hold values from 0.099609375 to 1.8984375
- mlp_gain: bfloat16 [1024], P(('narrow', 'wide')), may hold values from 0.099609375 to 1.8984375
- w_query: bfloat16 [1024, 1024], P(('narrow', 'wide')), may hold values from -0.1875 to 0.1875
- w_key: bfloat16 [1024, 1024], P(('narrow', 'wide')), may hold values from -0.1875 to 0.1875
- w_value: bfloat16 [1024, 1024], P(('narrow', 'wide')), may hold values from -0.1875 to 0.1875
- w_out: bfloat16 [1024, 1024], P(None, ('narrow', 'wide')), may hold values from -2 to 2
- w_gate: bfloat16 [1024, 2816], P('wide', 'narrow'), may hold values from -0.1875 to 0.1875
- w_up: bfloat16 [1024, 2816], P('wide', 'narrow'), may hold values from -0.1875 to 0.1875
- w_down: bfloat16 [2816, 1024], P('narrow', 'wide'), may hold values from -0.109375 to 0.109375
Outputs:
- layer_out: bfloat16 [16384, 1024], P(('narrow', 'wide'))
- in_grad: float32 [16384, 1024], P(('narrow', 'wide'))
- first_values_grad: float32 [16384, 1024], P(('narrow', 'wide'))
- attn_gain_grad: float32 [1024], P(('narrow', 'wide'))
- mlp_gain_grad: float32 [1024], P(('narrow', 'wide'))
- w_query_grad: float32 [1024, 1024], P(('narrow', 'wide'))
- w_key_grad: float32 [1024, 1024], P(('narrow', 'wide'))
- w_value_grad: float32 [1024, 1024], P(('narrow', 'wide'))
- w_out_grad: float32 [1024, 1024], P(None, ('narrow', 'wide'))
- w_gate_grad: float32 [1024, 2816], P('wide', 'narrow')
- w_up_grad: float32 [1024, 2816], P('wide', 'narrow')
- w_down_grad: float32 [2816, 1024], P('narrow', 'wide')
Inputs may be any that keep to these rules, and one draw needn't show every extreme that they name: `short_split`: used only in slots whose seq_group is 1.
All inputs are finite; a program needn't handle non-finite values.
Results may differ from a plain program's by a relative error of at most 0.014.
Values may be sent and summed in bfloat16 or wider, within the bound.
No kernel may reach another device: no remote copies, remote signals or barrier semaphores. Data moves between devices by JAX's collectives and lax.ppermute only.
A program may use at most 192 MiB of HBM per device.

v0:
```python
import math
import jax
import jax.numpy as jnp
from jax import lax
from jax.sharding import PartitionSpec as P

HEAD_DIM = 64
epsilon = 1e-06


def rms_scale(values):
    return lax.rsqrt(jnp.mean(values * values, axis=-1, keepdims=True) + epsilon)


def angles(positions, head_dim):
    half_dim = head_dim // 2
    frequency = jnp.exp(
        jnp.arange(half_dim, dtype=jnp.float32) * (-2.0 * math.log(10000.0) / head_dim)
    )
    turned = positions[:, None] * frequency[None, :]
    return (jnp.cos(turned)[:, None, :], jnp.sin(turned)[:, None, :])


def rotate(values, cos_table, sin_table):
    half_dim = values.shape[-1] // 2
    first_half = values[..., :half_dim]
    second_half = values[..., half_dim:]
    return jnp.concatenate(
        [
            first_half * cos_table - second_half * sin_table,
            second_half * cos_table + first_half * sin_table,
        ],
        axis=-1,
    )


def rotate_back(grads, cos_table, sin_table):
    half_dim = grads.shape[-1] // 2
    first_half = grads[..., :half_dim]
    second_half = grads[..., half_dim:]
    return jnp.concatenate(
        [
            first_half * cos_table + second_half * sin_table,
            second_half * cos_table - first_half * sin_table,
        ],
        axis=-1,
    )


def product(left, right):
    return jnp.dot(left, right, preferred_element_type=jnp.float32)


def norm_back(values, scale, gain_float, grad_normed):
    scaled = grad_normed * gain_float
    gain_grad = jnp.sum(grad_normed * values * scale, axis=0)
    grad_values = scale * scaled - values * (scale * scale * scale) * jnp.mean(
        scaled * values, axis=-1, keepdims=True
    )
    return (grad_values, gain_grad)


def silu_back(gate_proj, up_proj, grad_active):
    sigmoid_gate = jax.nn.sigmoid(gate_proj)
    grad_gate = (
        grad_active * up_proj * sigmoid_gate * (1.0 + gate_proj * (1.0 - sigmoid_gate))
    ).astype(jnp.bfloat16)
    grad_up = (grad_active * gate_proj * sigmoid_gate).astype(jnp.bfloat16)
    return (grad_gate, grad_up)


def on_device(
    layer_in,
    first_values,
    out_grad,
    seq_group,
    short_split,
    attn_gain,
    mlp_gain,
    w_query,
    w_key,
    w_value,
    w_out,
    w_gate,
    w_up,
    w_down,
):
    row_count, model_width = layer_in.shape
    head_dim = HEAD_DIM
    head_count = model_width // head_dim
    gain_attn, gain_mlp, full_query, full_key, full_value, full_out = (
        lax.all_gather(attn_gain, ("narrow", "wide"), axis=0, tiled=True),
        lax.all_gather(mlp_gain, ("narrow", "wide"), axis=0, tiled=True),
        lax.all_gather(w_query, ("narrow", "wide"), axis=0, tiled=True),
        lax.all_gather(w_key, ("narrow", "wide"), axis=0, tiled=True),
        lax.all_gather(w_value, ("narrow", "wide"), axis=0, tiled=True),
        lax.all_gather(w_out, ("narrow", "wide"), axis=1, tiled=True),
    )
    gate_cols, up_cols, down_rows = (
        lax.all_gather(w_gate, "wide", axis=0, tiled=True),
        lax.all_gather(w_up, "wide", axis=0, tiled=True),
        lax.all_gather(w_down, "wide", axis=1, tiled=True),
    )
    gain_attn = gain_attn.astype(jnp.float32)
    gain_mlp = gain_mlp.astype(jnp.float32)
    split_row = jnp.where(seq_group[0] == 0, row_count, short_split[0])
    row_index = jnp.arange(row_count, dtype=jnp.int32)
    second = row_index >= split_row
    positions = jnp.where(second, row_index - split_row, row_index).astype(jnp.float32)
    cos_table, sin_table = angles(positions, head_dim)
    input_rows = layer_in.astype(jnp.float32)
    scale_one = rms_scale(input_rows)
    normed = (input_rows * scale_one * gain_attn).astype(jnp.bfloat16)
    queries = rotate(
        product(normed, full_query).reshape(row_count, head_count, head_dim), cos_table, sin_table
    ).astype(jnp.bfloat16)
    key_rows = rotate(
        product(normed, full_key).reshape(row_count, head_count, head_dim), cos_table, sin_table
    ).astype(jnp.bfloat16)
    value_rows = (
        0.5 * product(normed, full_value) + 0.5 * first_values.astype(jnp.float32)
    ).astype(jnp.bfloat16)
    value_rows = value_rows.reshape(row_count, head_count, head_dim)
    block_rows = min(512, row_count)
    score_scale = head_dim ** (-0.5)

    def scores_for(row_block):
        query_start = row_block * block_rows
        key_end = query_start + block_rows
        raw_scores = (
            jnp.einsum("qhd,khd->hqk", queries, key_rows, preferred_element_type=jnp.float32)
            * score_scale
        )
        allowed = (second[query_start:key_end, None] == second[None, :key_end]) & (
            row_index[query_start:key_end, None] >= row_index[None, :key_end]
        )
        return jnp.where(allowed[None], raw_scores, -1e30)

    row_block = 0
    key_end = (row_block + 1) * block_rows
    scores = scores_for(row_block)
    row_max = jnp.max(scores, axis=-1, keepdims=True)
    exponent = jnp.exp(scores - row_max)
    row_sum = jnp.sum(exponent, axis=-1, keepdims=True)
    weights = (exponent / row_sum).astype(jnp.bfloat16)
    attended_parts = jnp.einsum(
        "hqk,khd->qhd", weights, value_rows, preferred_element_type=jnp.float32
    )
    log_sums = [row_max + jnp.log(row_sum)]
    attended = attended_parts.reshape(row_count, model_width).astype(jnp.bfloat16)
    hidden_in = input_rows + product(attended, full_out)
    scale_two = rms_scale(hidden_in)
    normed_two = (hidden_in * scale_two * gain_mlp).astype(jnp.bfloat16)
    gathered_rows = lax.all_gather(normed_two, "narrow", axis=0, tiled=True)
    gate_proj = product(gathered_rows, gate_cols)
    up_proj = product(gathered_rows, up_cols)
    active = (jax.nn.silu(gate_proj) * up_proj).astype(jnp.bfloat16)
    branch_out = lax.psum_scatter(
        product(active, down_rows).astype(jnp.bfloat16), "narrow", scatter_dimension=0, tiled=True
    ).astype(jnp.float32)
    grad_rows = lax.all_gather(out_grad, "narrow", axis=0, tiled=True)
    grad_active = product(grad_rows, down_rows.T)
    grad_down_w = product(active.T, grad_rows)
    grad_gate, grad_up = silu_back(gate_proj, up_proj, grad_active)
    grad_gate_w = product(gathered_rows.T, grad_gate)
    grad_up_w = product(gathered_rows.T, grad_up)
    grad_normed_two = lax.psum_scatter(
        product(grad_gate, gate_cols.T) + product(grad_up, up_cols.T),
        "narrow",
        scatter_dimension=0,
        tiled=True,
    )
    layer_out = (hidden_in + branch_out).astype(jnp.bfloat16)
    gate_grad, up_grad, down_grad = (
        lax.psum_scatter(
            grad_gate_w.astype(jnp.bfloat16), "wide", scatter_dimension=0, tiled=True
        ).astype(jnp.float32),
        lax.psum_scatter(
            grad_up_w.astype(jnp.bfloat16), "wide", scatter_dimension=0, tiled=True
        ).astype(jnp.float32),
        lax.psum_scatter(
            grad_down_w.astype(jnp.bfloat16), "wide", scatter_dimension=1, tiled=True
        ).astype(jnp.float32),
    )
    grad_norm_two, mlp_gain_part = norm_back(hidden_in, scale_two, gain_mlp, grad_normed_two)
    grad_hidden = out_grad.astype(jnp.float32) + grad_norm_two
    grad_branch = grad_hidden.astype(jnp.bfloat16)
    grad_out_w = product(attended.T, grad_branch)
    grad_attended = (
        product(grad_branch, full_out.T)
        .astype(jnp.bfloat16)
        .reshape(row_count, head_count, head_dim)
    )
    grad_keys = jnp.zeros((row_count, head_count, head_dim), jnp.float32)
    grad_values = jnp.zeros((row_count, head_count, head_dim), jnp.float32)
    row_block = 0
    query_start = row_block * block_rows
    key_end = query_start + block_rows
    scores = scores_for(row_block)
    probability = jnp.exp(scores - log_sums[row_block])
    grad_probs = jnp.einsum(
        "qhd,khd->hqk", grad_attended, value_rows, preferred_element_type=jnp.float32
    )
    delta_sum = jnp.sum(grad_probs * probability, axis=-1, keepdims=True)
    grad_scores = (score_scale * probability * (grad_probs - delta_sum)).astype(jnp.bfloat16)
    query_grad_parts = jnp.einsum(
        "hqk,khd->qhd", grad_scores, key_rows, preferred_element_type=jnp.float32
    )
    grad_keys = grad_keys.at[:key_end].add(
        jnp.einsum("hqk,qhd->khd", grad_scores, queries, preferred_element_type=jnp.float32)
    )
    grad_values = grad_values.at[:key_end].add(
        jnp.einsum(
            "hqk,qhd->khd",
            probability.astype(jnp.bfloat16),
            grad_attended,
            preferred_element_type=jnp.float32,
        )
    )
    grad_query_proj = (
        rotate_back(query_grad_parts, cos_table, sin_table)
        .reshape(row_count, model_width)
        .astype(jnp.bfloat16)
    )
    grad_key_proj = (
        rotate_back(grad_keys, cos_table, sin_table)
        .reshape(row_count, model_width)
        .astype(jnp.bfloat16)
    )
    values_grad = 0.5 * grad_values.reshape(row_count, model_width)
    grad_value_proj = values_grad.astype(jnp.bfloat16)
    grad_query_w = product(normed.T, grad_query_proj)
    grad_key_w = product(normed.T, grad_key_proj)
    grad_value_w = product(normed.T, grad_value_proj)
    grad_normed = (
        product(grad_query_proj, full_query.T)
        + product(grad_key_proj, full_key.T)
        + product(grad_value_proj, full_value.T)
    )
    grad_norm_one, attn_gain_part = norm_back(input_rows, scale_one, gain_attn, grad_normed)
    in_grad = grad_hidden + grad_norm_one
    attn_gain_grad, mlp_gain_grad, query_grad, key_grad, value_grad, out_proj_grad = (
        lax.psum_scatter(attn_gain_part, ("narrow", "wide"), scatter_dimension=0, tiled=True),
        lax.psum_scatter(mlp_gain_part, ("narrow", "wide"), scatter_dimension=0, tiled=True),
        lax.psum_scatter(grad_query_w, ("narrow", "wide"), scatter_dimension=0, tiled=True),
        lax.psum_scatter(grad_key_w, ("narrow", "wide"), scatter_dimension=0, tiled=True),
        lax.psum_scatter(grad_value_w, ("narrow", "wide"), scatter_dimension=0, tiled=True),
        lax.psum_scatter(grad_out_w, ("narrow", "wide"), scatter_dimension=1, tiled=True),
    )
    return (
        layer_out,
        in_grad,
        values_grad,
        attn_gain_grad,
        mlp_gain_grad,
        query_grad,
        key_grad,
        value_grad,
        out_proj_grad,
        gate_grad,
        up_grad,
        down_grad,
    )


def solution(mesh):
    placed = (
        P(("narrow", "wide"), None),
        P(("narrow", "wide"), None),
        P(("narrow", "wide"), None),
        P(("narrow", "wide")),
        P(("narrow", "wide")),
        P(("narrow", "wide")),
        P(("narrow", "wide")),
        P(("narrow", "wide"), None),
        P(("narrow", "wide"), None),
        P(("narrow", "wide"), None),
        P(None, ("narrow", "wide")),
        P("wide", "narrow"),
        P("wide", "narrow"),
        P("narrow", "wide"),
    )
    return jax.shard_map(
        on_device,
        mesh=mesh,
        in_specs=placed,
        out_specs=(
            P(("narrow", "wide"), None),
            P(("narrow", "wide"), None),
            P(("narrow", "wide"), None),
            P(("narrow", "wide")),
            P(("narrow", "wide")),
            P(("narrow", "wide"), None),
            P(("narrow", "wide"), None),
            P(("narrow", "wide"), None),
            P(None, ("narrow", "wide")),
            P("wide", "narrow"),
            P("wide", "narrow"),
            P("narrow", "wide"),
        ),
        check_vma=False,
    )
```

profile of v0, /device:TPU:0, one launch (start us, length us, event | category | flops | bytes accessed | tf_op | source)
XLA Modules:
  0.0 1429.1 jit_solution(4299515157416208333)
XLA Ops:
  15.2 42.0 %all-reduce.5 = (bf16[1024]{0:T(1024)(128)(2,1)S(1)}, bf16[1024]{0:T(1024)(128)(2,1)S(1)}) all-reduce(bf16[1024]{0:T(1024)(128)(2,1)S(1)} %dynamic-update-slice.4, bf16[1024]{0:T(1024)(128)(2,1)S(1)} %dynamic-update-slice.5), channel_id=1, replica_groups=mesh['narrow'=4,'wide'=8] {'narrow','wide'}, use_global_device_ids=true, to_apply=%add | all-reduce | flops 2048 | bytes 8192
  58.3 11.8 all-gather.10.cloned.1.call-done
  70.1 3.6 multiply_convert_fusion.5
  74.2 54.0 %all-gather.12.cloned.1.call-done = bf16[1024,1024]{1,0:T(8,128)(2,1)} async-done(((bf16[32,1024]{1,0:T(8,128)(2,1)}), bf16[1024,1024]{1,0:T(8,128)(2,1)}) %all-gather.12.cloned.1.call-update) | async-done | bytes 2097168 | tf_op jit(solution)/shard_map/all_gather | solution.py:94
  128.2 4.3 fusion.36
  132.5 53.8 %all-gather.14.cloned.1.call-done = bf16[1024,1024]{1,0:T(8,128)(2,1)} async-done(((bf16[32,1024]{1,0:T(8,128)(2,1)}), bf16[1024,1024]{1,0:T(8,128)(2,1)}) %all-gather.14.cloned.1.call-update) | async-done | bytes 2097168 | tf_op jit(solution)/shard_map/all_gather | solution.py:95
  186.3 3.1 fusion.34
  190.2 7.4 fusion.39
  197.7 8.3 fusion
  205.9 8.7 fusion.18
  214.6 29.7 %all-gather.16.cloned.1.call-done = bf16[1024,1024]{0,1:T(8,128)(2,1)} async-done(((bf16[1024,32]{0,1:T(8,128)(2,1)}), bf16[1024,1024]{0,1:T(8,128)(2,1)}) %all-gather.16.cloned.1.call-update) | async-done | bytes 2097168 | tf_op jit(solution)/shard_map/all_gather | solution.py:97
  244.3 3.3 multiply_reduce_fusion.3
  251.3 18.9 %all-gather.22.cloned.1.call-done = bf16[1024,704]{0,1:T(8,128)(2,1)} async-done(((bf16[128,704]{0,1:T(8,128)(2,1)}), bf16[1024,704]{0,1:T(8,128)(2,1)}) %all-gather.22.cloned.1.call-update) | async-done | bytes 1441808 | tf_op jit(solution)/shard_map/all_gather | solution.py:101
  270.2 82.8 %all-gather.18.cloned.1.call-done = bf16[2048,1024]{1,0:T(8,128)(2,1)} async-done(((bf16[512,1024]{1,0:T(8,128)(2,1)}), bf16[2048,1024]{1,0:T(8,128)(2,1)}) %all-gather.18.cloned.1.call-update) | async-done | bytes 4194320 | tf_op jit(solution)/shard_map/all_gather | solution.py:154
  353.0 8.3 fusion.41
  361.3 17.4 %all-gather.20.cloned.1.call-done = bf16[1024,704]{0,1:T(8,128)(2,1)} async-done(((bf16[128,704]{0,1:T(8,128)(2,1)}), bf16[1024,704]{0,1:T(8,128)(2,1)}) %all-gather.20.cloned.1.call-update) | async-done | bytes 1441808 | tf_op jit(solution)/shard_map/all_gather | solution.py:100
  378.7 8.3 fusion.40
  387.0 18.9 %all-gather.24.cloned.1.call-done = bf16[704,1024]{1,0:T(8,128)(2,1)} async-done(((bf16[704,128]{1,0:T(8,128)(2,1)}), bf16[704,1024]{1,0:T(8,128)(2,1)}) %all-gather.24.cloned.1.call-update) | async-done | bytes 1441808 | tf_op jit(solution)/shard_map/all_gather | solution.py:102
  405.9 82.4 %all-gather.26.cloned.1.call-done = bf16[2048,1024]{1,0:T(8,128)(2,1)} async-done(((bf16[512,1024]{1,0:T(8,128)(2,1)}), bf16[2048,1024]{1,0:T(8,128)(2,1)}) %all-gather.26.cloned.1.call-update) | async-done | bytes 4194320 | tf_op jit(solution)/shard_map/all_gather | solution.py:161
  488.3 12.1 multiply_convert_fusion.1
  500.4 3.5 fusion.42
  504.0 5.8 convolution_add_fusion
  509.9 7.7 convolution_convert_fusion
  517.8 7.3 convolution_convert_fusion.3
  527.7 7.4 convolution_convert_fusion.1
  537.8 7.3 convolution_convert_fusion.2
  547.7 105.2 %reduce-scatter.18.cloned.1.call-done = f32[512,1024]{1,0:T(8,128)} async-done(((f32[2048,1024]{1,0:T(8,128)}), f32[512,1024]{1,0:T(8,128)}) %reduce-scatter.18.cloned.1.call-update) | async-done | bytes 2097168 | tf_op jit(solution)/shard_map/reduce_scatter | solution.py:167
  655.1 77.7 %reduce-scatter.16.cloned.1.call-done = bf16[512,1024]{1,0:T(8,128)(2,1)} async-done(((bf16[2048,1024]{1,0:T(8,128)(2,1)}), bf16[512,1024]{1,0:T(8,128)(2,1)}) %reduce-scatter.16.cloned.1.call-update) | async-done | bytes 1048592 | tf_op jit(solution)/shard_map/reduce_scatter | solution.py:158
  732.8 4.5 subtract_add_fusion
  737.3 3.3 fusion.23
  740.9 3.9 convolution_convert_fusion.4
  746.4 7.8 fusion.15
  755.5 3.5 fusion.20
  759.1 8.5 multiply_reduce_fusion
  767.6 8.4 multiply_convert_fusion
  776.0 3.7 convolution_bitcast_fusion
  783.7 3.4 fusion.32
  787.5 3.5 fusion.30
  793.0 24.4 %reduce-scatter.30.cloned.1.call-done = bf16[128,704]{1,0:T(8,128)(2,1)} async-done(((bf16[1024,704]{1,0:T(8,128)(2,1)}), bf16[128,704]{1,0:T(8,128)(2,1)}) %reduce-scatter.30.cloned.1.call-update) | async-done | bytes 180240
  819.3 40.1 %reduce-scatter.28.cloned.1.call-done = bf16[128,704]{1,0:T(8,128)(2,1)} async-done(((bf16[1024,704]{1,0:T(8,128)(2,1)}), bf16[128,704]{1,0:T(8,128)(2,1)}) %reduce-scatter.28.cloned.1.call-update) | async-done | bytes 180240
  863.1 3.4 fusion.44
  868.1 3.2 fusion.14
  871.2 39.8 %all-reduce.4 = (f32[1024]{0:T(1024)S(1)}, f32[1024]{0:T(1024)S(1)}) all-reduce(f32[1024]{0:T(1024)S(1)} %get-tuple-element.90, f32[1024]{0:T(1024)S(1)} %get-tuple-element.88), channel_id=4, replica_groups=mesh['narrow'=4,'wide'=8] {'narrow','wide'}, use_global_device_ids=true, to_apply=%region_10.11.clone | all-reduce | flops 2048 | bytes 16384
  912.2 4.1 fusion.11
  916.3 86.8 %reduce-scatter.26.cloned.1.call-done = f32[1024,32]{0,1:T(8,128)} async-done(((f32[1024,1024]{0,1:T(8,128)}), f32[1024,32]{0,1:T(8,128)}) %reduce-scatter.26.cloned.1.call-update) | async-done | bytes 131088 | tf_op jit(solution)/shard_map/reduce_scatter | solution.py:248
  1003.1 139.6 %reduce-scatter.24.cloned.1.call-done = f32[32,1024]{1,0:T(8,128)} async-done(((f32[1024,1024]{1,0:T(8,128)}), f32[32,1024]{1,0:T(8,128)}) %reduce-scatter.24.cloned.1.call-update) | async-done | bytes 131088 | tf_op jit(solution)/shard_map/reduce_scatter | solution.py:247
  1142.7 139.6 %reduce-scatter.20.cloned.1.call-done = f32[32,1024]{1,0:T(8,128)} async-done(((f32[1024,1024]{1,0:T(8,128)}), f32[32,1024]{1,0:T(8,128)}) %reduce-scatter.20.cloned.1.call-update) | async-done | bytes 131088 | tf_op jit(solution)/shard_map/reduce_scatter | solution.py:245
  1282.3 139.5 %reduce-scatter.22.cloned.1.call-done = f32[32,1024]{1,0:T(8,128)} async-done(((f32[1024,1024]{1,0:T(8,128)}), f32[32,1024]{1,0:T(8,128)}) %reduce-scatter.22.cloned.1.call-update) | async-done | bytes 131088 | tf_op jit(solution)/shard_map/reduce_scatter | solution.py:246
  (137 shorter events, 40.6 us)
Async XLA Ops:
  7.2 62.9 %all-gather.10.cloned.1.call-start = ((), (), s32[]{:S(2)}) async-start(), calls=%async_computation.9 | async-start | bytes 2162688 | tf_op jit(solution)/shard_map/all_gather | solution.py:96
  7.9 120.3 %all-gather.12.cloned.1.call-start = ((), (), s32[]{:S(2)}) async-start(), calls=%async_computation.10 | async-start | bytes 2162688 | tf_op jit(solution)/shard_map/all_gather | solution.py:94
  8.7 177.6 %all-gather.14.cloned.1.call-start = ((), (), s32[]{:S(2)}) async-start(), calls=%async_computation.11 | async-start | bytes 2162688 | tf_op jit(solution)/shard_map/all_gather | solution.py:95
  9.4 234.9 %all-gather.16.cloned.1.call-start = ((), (), s32[]{:S(2)}) async-start(), calls=%async_computation.12 | async-start | bytes 2162688 | tf_op jit(solution)/shard_map/all_gather | solution.py:97
  10.0 260.2 %all-gather.22.cloned.1.call-start = ((), (), s32[]{:S(2)}) async-start(), calls=%async_computation.15 | async-start | bytes 1622016 | tf_op jit(solution)/shard_map/all_gather | solution.py:101
  10.6 342.4 %all-gather.18.cloned.1.call-start = ((), (), s32[]{:S(2)}) async-start(), calls=%async_computation.13 | async-start | bytes 5242880 | tf_op jit(solution)/shard_map/all_gather | solution.py:154
  58.3 131.2 %copy-start.21 = (f32[512,32]{0,1:T(8,128)}, f32[512,32]{0,1:T(8,128)S(1)}, u32[]{:S(2)}) copy-start(f32[512,32]{0,1:T(8,128)S(1)} %get-tuple-element.113) | copy-start | bytes 196612
  58.3 131.2 %copy-start.23 = (f32[512,32]{0,1:T(8,128)}, f32[512,32]{0,1:T(8,128)S(1)}, u32[]{:S(2)}) copy-start(f32[512,32]{0,1:T(8,128)S(1)} %get-tuple-element.114) | copy-start | bytes 196612
  70.1 58.1 %copy-start.2 = (bf16[512,1024]{1,0:T(8,128)(2,1)S(1)}, bf16[512,1024]{1,0:T(8,128)(2,1)}, u32[]{:S(2)}) copy-start(bf16[512,1024]{1,0:T(8,128)(2,1)} %param.22) | copy-start | bytes 3145732
  74.2 131.8 %copy-start.7 = (bf16[512,1024]{0,1:T(8,128)(2,1)}, bf16[512,1024]{0,1:T(8,128)(2,1)S(1)}, u32[]{:S(2)}) copy-start(bf16[512,1024]{0,1:T(8,128)(2,1)S(1)} %copy.48) | copy-start | bytes 3145732
  186.3 3.2 copy-start.9
  190.2 7.4 copy-start.10
  190.2 7.4 copy-start.12
  190.2 7.4 copy-start.14
  190.2 7.4 copy-start.16
  247.6 405.4 %copy-start.5 = (f32[512,1024]{1,0:T(8,128)}, f32[512,1024]{1,0:T(8,128)S(1)}, u32[]{:S(2)}) copy-start(f32[512,1024]{1,0:T(8,128)S(1)} %get-tuple-element.122) | copy-start | bytes 6291460
  249.0 129.7 %all-gather.20.cloned.1.call-start = ((), (), s32[]{:S(2)}) async-start(), calls=%async_computation.14 | async-start | bytes 1622016 | tf_op jit(solution)/shard_map/all_gather | solution.py:100
  249.8 156.1 %all-gather.24.cloned.1.call-start = ((), (), s32[]{:S(2)}) async-start(), calls=%async_computation.16 | async-start | bytes 1622016 | tf_op jit(solution)/shard_map/all_gather | solution.py:102
  250.5 237.8 %all-gather.26.cloned.1.call-start = ((), (), s32[]{:S(2)}) async-start(), calls=%async_computation.18 | async-start | bytes 5242880 | tf_op jit(solution)/shard_map/all_gather | solution.py:161
  251.3 401.7 %reduce-scatter.18.cloned.1.call-start = ((), (), s32[]{:S(2)}) async-start(), calls=%async_computation.19 | async-start | bytes 10485760 | tf_op jit(solution)/shard_map/reduce_scatter | solution.py:167
  488.3 12.1 copy-start.28
  500.4 3.5 copy-start.30
  500.4 3.5 copy-start.29
  500.4 3.5 copy-start.27
  509.8 223.0 %reduce-scatter.16.cloned.1.call-start = ((), (), s32[]{:S(2)}) async-start(), calls=%async_computation.17 | async-start | bytes 5242880 | tf_op jit(solution)/shard_map/reduce_scatter | solution.py:158
  517.5 273.5 %reduce-scatter.32.cloned.1.call-start = ((), (), s32[]{:S(2)}) async-start(), calls=%async_computation.26 | async-start | bytes 1769472
  527.7 289.8 %reduce-scatter.30.cloned.1.call-start = ((), (), s32[]{:S(2)}) async-start(), calls=%async_computation.25 | async-start | bytes 1769472
  537.7 321.7 %reduce-scatter.28.cloned.1.call-start = ((), (), s32[]{:S(2)}) async-start(), calls=%async_computation.24 | async-start | bytes 1769472
  547.7 455.4 %reduce-scatter.26.cloned.1.call-start = ((), (), s32[]{:S(2)}) async-start(), calls=%async_computation.23 | async-start | bytes 4325376 | tf_op jit(solution)/shard_map/reduce_scatter | solution.py:248
  732.8 4.5 copy-start.8
  737.3 3.6 copy-start.4
  740.6 402.0 %reduce-scatter.24.cloned.1.call-start = ((), (), s32[]{:S(2)}) async-start(), calls=%async_computation.22 | async-start | bytes 4325376 | tf_op jit(solution)/shard_map/reduce_scatter | solution.py:247
  746.4 7.8 copy-start.6
  754.2 1.3 copy-start
  759.1 523.3 %reduce-scatter.20.cloned.1.call-start = ((), (), s32[]{:S(2)}) async-start(), calls=%async_computation.20 | async-start | bytes 4325376 | tf_op jit(solution)/shard_map/reduce_scatter | solution.py:245
  767.6 8.4 copy-start.15
  776.0 3.8 copy-start.11
  776.0 3.8 copy-start.13
  779.8 1.6 copy-start.22
  779.8 1.6 copy-start.24
  782.1 1.6 copy-start.3
  782.3 5.2 copy-start.20
  787.1 634.7 %reduce-scatter.22.cloned.1.call-start = ((), (), s32[]{:S(2)}) async-start(), calls=%async_computation.21 | async-start | bytes 4325376 | tf_op jit(solution)/shard_map/reduce_scatter | solution.py:246
  791.0 70.3 %copy-start.1 = (f32[16,64,512]{2,1,0:T(8,128)S(1)}, f32[16,64,512]{2,1,0:T(8,128)}, u32[]{:S(2)}) copy-start(f32[16,64,512]{2,1,0:T(8,128)} %copy-done) | copy-start | bytes 6291460
  863.1 3.4 copy-start.19
  863.1 3.4 copy-start.26
  866.5 1.6 copy-start.17
  868.1 44.2 %copy-start.25 = (f32[512]{0:T(512)S(1)}, f32[512]{0:T(512)}, u32[]{:S(2)}) copy-start(f32[512]{0:T(512)} %get-tuple-element.115) | copy-start | bytes 6148
  (1 other events, 1.0 us)
Sparse Core Ops, SparseCore 0:
  10.9 59.1 all-gather.9
  72.9 55.2 all-gather.11
  131.0 55.2 all-gather.13
  189.0 55.2 all-gather.15
  246.0 24.1 all-gather.21
  272.2 80.7 all-gather.17
  354.9 23.8 all-gather.19
  380.6 25.2 all-gather.23
  407.5 80.7 all-gather.25
  509.9 142.9 reduce-scatter.17
  655.3 77.4 reduce-scatter.15
  736.3 38.9 reduce-scatter.31
  778.9 38.4 reduce-scatter.29
  820.9 38.4 reduce-scatter.27
  862.2 140.8 reduce-scatter.25
  1005.9 136.7 reduce-scatter.23
  1145.5 136.8 reduce-scatter.19
  1285.1 136.6 reduce-scatter.21
where the time goes:
time: 1440 us; the launch traced here: 1430 us
  waiting for transfers between devices  1130 us (78%)
  matrix products  145 us (10%)
  blocking collectives  81.8 us (6%)
  other arithmetic  35.4 us (2%)
  local copies, waits for them, and re-layouts  21 us (1%)
  between operations  16.6 us (1%)
    reduce_scatter x1, waiting for transfers between devices, on_device(): lax.psum_scatter(grad_query_w, ('narrow', 'wide'), scatter_dimension=0, t...  140 us
    reduce_scatter x1, waiting for transfers between devices, on_device(): lax.psum_scatter(grad_value_w, ('narrow', 'wide'), scatter_dimension=0, t...  140 us
    reduce_scatter x1, waiting for transfers between devices, on_device(): lax.psum_scatter(grad_key_w, ('narrow', 'wide'), scatter_dimension=0, til...  139 us
    dot_general x21, matrix products, product(): return jnp.dot(left, right, preferred_element_type=jnp.float32)  107 us
    reduce_scatter x1, waiting for transfers between devices, on_device(): lax.psum_scatter(product(grad_gate, gate_cols.T) + product(grad_up, up_co...  105 us
    reduce_scatter x1, waiting for transfers between devices, on_device(): lax.psum_scatter(grad_out_w, ('narrow', 'wide'), scatter_dimension=1, til...  86.8 us
    all_gather x1, waiting for transfers between devices, on_device(): gathered_rows = lax.all_gather(normed_two, 'narrow', axis=0, tiled=True)  82.8 us
    all_gather x1, waiting for transfers between devices, on_device(): grad_rows = lax.all_gather(out_grad, 'narrow', axis=0, tiled=True)  82.4 us
  transfers between devices with their start and end apart: 18, of which 17 were waited for; matrix products, arithmetic and copies ran while one was open for 12% of the time, Pallas kernels for 0%

commit v1 on v0

--- a/solution.py
+++ b/solution.py
@@ -6,6 +6,28 @@
 
 HEAD_DIM = 64
 epsilon = 1e-06
+
+
+def in_order(blocks, dim):
+    blocks = jnp.moveaxis(blocks, 0, dim)
+    lengths = blocks.shape
+    return blocks.reshape(*lengths[:dim], lengths[dim] * lengths[dim + 1], *lengths[dim + 2 :])
+
+
+def collect(x, axis, dim):
+    size = lax.axis_size(axis)
+    pairs = [(i, (i + 1) % size) for i in range(size)]
+    back = [(b, a) for a, b in pairs]
+    lower, upper = ([], [])
+    for step in range(size - 1):
+        if step % 2 == 0:
+            lower.append(lax.ppermute(lower[-1] if lower else x, axis, pairs))
+        else:
+            upper.append(lax.ppermute(upper[-1] if upper else x, axis, back))
+    parts = jnp.stack([*lower[::-1], x, *upper])
+    shift = lax.axis_index(axis) - len(lower)
+    parts = parts[(jnp.arange(size) - shift) % size]
+    return in_order(parts, dim)
 
 
 def rms_scale(values):
@@ -158,7 +180,7 @@
     branch_out = lax.psum_scatter(
         product(active, down_rows).astype(jnp.bfloat16), "narrow", scatter_dimension=0, tiled=True
     ).astype(jnp.float32)
-    grad_rows = lax.all_gather(out_grad, "narrow", axis=0, tiled=True)
+    grad_rows = collect(out_grad, "narrow", 0)
     grad_active = product(grad_rows, down_rows.T)
     grad_down_w = product(active.T, grad_rows)
     grad_gate, grad_up = silu_back(gate_proj, up_proj, grad_active)

time: 1440 us -> 1390 us (0.965)
  waiting for transfers between devices: 1130 us -> 1070 us
    ppermute x0 -> x3, waiting for transfers between devices: none -> 106 us  [the longest x1 65.8 us: collect(): upper.append(lax.ppermute(upper[-1] if upper else x, axis, back))]
    all_gather x1 -> x0, waiting for transfers between devices: 82.4 us -> none  [on_device(): grad_rows = lax.all_gather(out_grad, 'narrow', axis=0, tiled=True)]
    all_gather x1, waiting for transfers between devices: 82.8 us -> 20.4 us  [on_device(): gathered_rows = lax.all_gather(normed_two, 'narrow', axis=0, tiled=True)]
    all_gather x1, waiting for transfers between devices: 18.9 us -> 0.01 us  [on_device(): lax.all_gather(w_up, 'wide', axis=0, tiled=True)]
    unnamed x21 -> x20, waiting for transfers between devices: 69.9 us -> 68.3 us
  transfers between devices with their start and end apart: 18 -> 20, of which waited for: 17 -> 18; matrix products, arithmetic and copies ran while one was open for 12% -> 13% of each run, Pallas kernels for 0% -> 0%
where the time goes in v1:
time: 1390 us; the launch traced here: 1380 us
  waiting for transfers between devices  1070 us (77%)
  matrix products  146 us (11%)
  blocking collectives  81.7 us (6%)
  other arithmetic  39.1 us (3%)
  local copies, waits for them, and re-layouts  25 us (2%)
  between operations  16.3 us (1%)
    reduce_scatter x1, waiting for transfers between devices, on_device(): lax.psum_scatter(grad_query_w, ('narrow', 'wide'), scatter_dimension=0, t...  140 us
    reduce_scatter x1, waiting for transfers between devices, on_device(): lax.psum_scatter(grad_key_w, ('narrow', 'wide'), scatter_dimension=0, til...  140 us
    reduce_scatter x1, waiting for transfers between devices, on_device(): lax.psum_scatter(grad_value_w, ('narrow', 'wide'), scatter_dimension=0, t...  140 us
    dot_general x21, matrix products, product(): return jnp.dot(left, right, preferred_element_type=jnp.float32)  109 us
    reduce_scatter x1, waiting for transfers between devices, on_device(): lax.psum_scatter(product(grad_gate, gate_cols.T) + product(grad_up, up_co...  107 us
    reduce_scatter x1, waiting for transfers between devices, on_device(): lax.psum_scatter(grad_out_w, ('narrow', 'wide'), scatter_dimension=1, til...  87 us
    unnamed x2, blocking collectives  81.7 us
    reduce_scatter x1, waiting for transfers between devices, on_device(): lax.psum_scatter(product(active, down_rows).astype(jnp.bfloat16), 'narrow...  77.5 us
  transfers between devices with their start and end apart: 20, of which 18 were waited for; matrix products, arithmetic and copies ran while one was open for 13% of the time, Pallas kernels for 0%

profile of v1, /device:TPU:0, one launch (start us, length us, event | category | flops | bytes accessed | tf_op | source)
XLA Modules:
  0.0 1384.3 jit_solution(16154939046078821957)
XLA Ops:
  15.2 42.0 %all-reduce.5 = (bf16[1024]{0:T(1024)(128)(2,1)S(1)}, bf16[1024]{0:T(1024)(128)(2,1)S(1)}) all-reduce(bf16[1024]{0:T(1024)(128)(2,1)S(1)} %dynamic-update-slice.4, bf16[1024]{0:T(1024)(128)(2,1)S(1)} %dynamic-update-slice.5), channel_id=1, replica_groups=mesh['narrow'=4,'wide'=8] {'narrow','wide'}, use_global_device_ids=true, to_apply=%add | all-reduce | flops 2048 | bytes 8192
  58.3 11.8 all-gather.9.cloned.1.call-done
  70.1 3.6 multiply_convert_fusion.5
  74.2 54.0 %all-gather.11.cloned.1.call-done = bf16[1024,1024]{1,0:T(8,128)(2,1)} async-done(((bf16[32,1024]{1,0:T(8,128)(2,1)}), bf16[1024,1024]{1,0:T(8,128)(2,1)}) %all-gather.11.cloned.1.call-update) | async-done | bytes 2097168 | tf_op jit(solution)/shard_map/all_gather | solution.py:116
  128.2 4.3 fusion.38
  132.5 53.8 %all-gather.13.cloned.1.call-done = bf16[1024,1024]{1,0:T(8,128)(2,1)} async-done(((bf16[32,1024]{1,0:T(8,128)(2,1)}), bf16[1024,1024]{1,0:T(8,128)(2,1)}) %all-gather.13.cloned.1.call-update) | async-done | bytes 2097168 | tf_op jit(solution)/shard_map/all_gather | solution.py:117
  190.2 7.4 fusion.41
  197.7 8.3 fusion
  205.9 8.8 fusion.18
  214.8 29.5 %all-gather.15.cloned.1.call-done = bf16[1024,1024]{0,1:T(8,128)(2,1)} async-done(((bf16[1024,32]{0,1:T(8,128)(2,1)}), bf16[1024,1024]{0,1:T(8,128)(2,1)}) %all-gather.15.cloned.1.call-update) | async-done | bytes 2097168 | tf_op jit(solution)/shard_map/all_gather | solution.py:119
  253.5 24.3 %collective-permute-done = bf16[512,1024]{1,0:T(8,128)(2,1)} collective-permute-done((bf16[512,1024]{1,0:T(8,128)(2,1)}, bf16[512,1024]{1,0:T(8,128)(2,1)}, u32[]{:S(2)}, u32[]{:S(2)}) %collective-permute-start) | collective-permute-done | bytes 1048608 | tf_op jit(solution)/shard_map/ppermute | solution.py:24
  278.0 65.8 %collective-permute-done.2 = bf16[512,1024]{1,0:T(8,128)(2,1)} collective-permute-done((bf16[512,1024]{1,0:T(8,128)(2,1)}, bf16[512,1024]{1,0:T(8,128)(2,1)}, u32[]{:S(2)}, u32[]{:S(2)}) %collective-permute-start.2) | collective-permute-done | bytes 1048608 | tf_op jit(solution)/shard_map/ppermute | solution.py:26
  343.8 15.9 %collective-permute-done.1 = bf16[512,1024]{1,0:T(8,128)(2,1)} collective-permute-done((bf16[512,1024]{1,0:T(8,128)(2,1)}, bf16[512,1024]{1,0:T(8,128)(2,1)}, u32[]{:S(2)}, u32[]{:S(2)}) %collective-permute-start.1) | collective-permute-done | bytes 1048608 | tf_op jit(solution)/shard_map/ppermute | solution.py:24
  359.7 3.8 pad_maximum_fusion
  363.5 5.0 gather_fusion
  368.5 20.4 %all-gather.17.cloned.1.call-done = bf16[2048,1024]{1,0:T(8,128)(2,1)} async-done(((bf16[512,1024]{1,0:T(8,128)(2,1)}), bf16[2048,1024]{1,0:T(8,128)(2,1)}) %all-gather.17.cloned.1.call-update) | async-done | bytes 4194320 | tf_op jit(solution)/shard_map/all_gather | solution.py:176
  388.9 8.3 fusion.43
  397.2 17.4 %all-gather.19.cloned.1.call-done = bf16[1024,704]{0,1:T(8,128)(2,1)} async-done(((bf16[128,704]{0,1:T(8,128)(2,1)}), bf16[1024,704]{0,1:T(8,128)(2,1)}) %all-gather.19.cloned.1.call-update) | async-done | bytes 1441808 | tf_op jit(solution)/shard_map/all_gather | solution.py:122
  414.6 8.3 fusion.42
  422.9 18.9 %all-gather.23.cloned.1.call-done = bf16[704,1024]{1,0:T(8,128)(2,1)} async-done(((bf16[704,128]{1,0:T(8,128)(2,1)}), bf16[704,1024]{1,0:T(8,128)(2,1)}) %all-gather.23.cloned.1.call-update) | async-done | bytes 1441808 | tf_op jit(solution)/shard_map/all_gather | solution.py:124
  441.8 11.8 multiply_convert_fusion.1
  453.6 3.5 fusion.44
  457.1 6.0 convolution_add_fusion
  463.2 7.7 convolution_convert_fusion
  471.0 7.3 convolution_convert_fusion.3
  480.9 7.3 convolution_convert_fusion.1
  491.1 7.3 convolution_convert_fusion.2
  501.0 106.8 %reduce-scatter.18.cloned.1.call-done = f32[512,1024]{1,0:T(8,128)} async-done(((f32[2048,1024]{1,0:T(8,128)}), f32[512,1024]{1,0:T(8,128)}) %reduce-scatter.18.cloned.1.call-update) | async-done | bytes 2097168 | tf_op jit(solution)/shard_map/reduce_scatter | solution.py:189
  609.9 77.5 %reduce-scatter.16.cloned.1.call-done = bf16[512,1024]{1,0:T(8,128)(2,1)} async-done(((bf16[2048,1024]{1,0:T(8,128)(2,1)}), bf16[512,1024]{1,0:T(8,128)(2,1)}) %reduce-scatter.16.cloned.1.call-update) | async-done | bytes 1048592 | tf_op jit(solution)/shard_map/reduce_scatter | solution.py:180
  687.5 4.6 subtract_add_fusion
  692.1 4.9 fusion.23
  697.1 3.6 convolution_convert_fusion.4
  701.2 7.8 fusion.15
  710.4 3.5 fusion.20
  714.2 8.5 multiply_reduce_fusion
  722.6 8.4 multiply_convert_fusion
  731.1 3.8 convolution_bitcast_fusion
  738.8 3.4 fusion.34
  742.6 3.5 fusion.32
  748.1 24.0 %reduce-scatter.30.cloned.1.call-done = bf16[128,704]{1,0:T(8,128)(2,1)} async-done(((bf16[1024,704]{1,0:T(8,128)(2,1)}), bf16[128,704]{1,0:T(8,128)(2,1)}) %reduce-scatter.30.cloned.1.call-update) | async-done | bytes 180240
  774.0 40.3 %reduce-scatter.28.cloned.1.call-done = bf16[128,704]{1,0:T(8,128)(2,1)} async-done(((bf16[1024,704]{1,0:T(8,128)(2,1)}), bf16[128,704]{1,0:T(8,128)(2,1)}) %reduce-scatter.28.cloned.1.call-update) | async-done | bytes 180240
  817.9 3.4 fusion.46
  826.1 39.8 %all-reduce.4 = (f32[1024]{0:T(1024)S(1)}, f32[1024]{0:T(1024)S(1)}) all-reduce(f32[1024]{0:T(1024)S(1)} %get-tuple-element.90, f32[1024]{0:T(1024)S(1)} %get-tuple-element.88), channel_id=4, replica_groups=mesh['narrow'=4,'wide'=8] {'narrow','wide'}, use_global_device_ids=true, to_apply=%region_10.11.clone | all-reduce | flops 2048 | bytes 16384
  867.0 4.1 fusion.11
  871.1 87.0 %reduce-scatter.26.cloned.1.call-done = f32[1024,32]{0,1:T(8,128)} async-done(((f32[1024,1024]{0,1:T(8,128)}), f32[1024,32]{0,1:T(8,128)}) %reduce-scatter.26.cloned.1.call-update) | async-done | bytes 131088 | tf_op jit(solution)/shard_map/reduce_scatter | solution.py:270
  958.2 139.5 %reduce-scatter.24.cloned.1.call-done = f32[32,1024]{1,0:T(8,128)} async-done(((f32[1024,1024]{1,0:T(8,128)}), f32[32,1024]{1,0:T(8,128)}) %reduce-scatter.24.cloned.1.call-update) | async-done | bytes 131088 | tf_op jit(solution)/shard_map/reduce_scatter | solution.py:269
  1097.7 139.8 %reduce-scatter.20.cloned.1.call-done = f32[32,1024]{1,0:T(8,128)} async-done(((f32[1024,1024]{1,0:T(8,128)}), f32[32,1024]{1,0:T(8,128)}) %reduce-scatter.20.cloned.1.call-update) | async-done | bytes 131088 | tf_op jit(solution)/shard_map/reduce_scatter | solution.py:267
  1237.6 139.7 %reduce-scatter.22.cloned.1.call-done = f32[32,1024]{1,0:T(8,128)} async-done(((f32[1024,1024]{1,0:T(8,128)}), f32[32,1024]{1,0:T(8,128)}) %reduce-scatter.22.cloned.1.call-update) | async-done | bytes 131088 | tf_op jit(solution)/shard_map/reduce_scatter | solution.py:268
  (140 shorter events, 51.8 us)
Async XLA Ops:
  7.2 62.9 %all-gather.9.cloned.1.call-start = ((), (), s32[]{:S(2)}) async-start(), calls=%async_computation.9 | async-start | bytes 2162688 | tf_op jit(solution)/shard_map/all_gather | solution.py:118
  7.9 120.3 %all-gather.11.cloned.1.call-start = ((), (), s32[]{:S(2)}) async-start(), calls=%async_computation.10 | async-start | bytes 2162688 | tf_op jit(solution)/shard_map/all_gather | solution.py:116
  8.7 177.7 %all-gather.13.cloned.1.call-start = ((), (), s32[]{:S(2)}) async-start(), calls=%async_computation.11 | async-start | bytes 2162688 | tf_op jit(solution)/shard_map/all_gather | solution.py:117
  9.4 234.9 %all-gather.15.cloned.1.call-start = ((), (), s32[]{:S(2)}) async-start(), calls=%async_computation.12 | async-start | bytes 2162688 | tf_op jit(solution)/shard_map/all_gather | solution.py:119
  10.0 358.6 %all-gather.21.cloned.1.call-start = ((), (), s32[]{:S(2)}) async-start(), calls=%async_computation.15 | async-start | bytes 1622016 | tf_op jit(solution)/shard_map/all_gather | solution.py:123
  10.6 378.4 %all-gather.17.cloned.1.call-start = ((), (), s32[]{:S(2)}) async-start(), calls=%async_computation.13 | async-start | bytes 5242880 | tf_op jit(solution)/shard_map/all_gather | solution.py:176
  58.3 131.2 %copy-start.19 = (f32[512,32]{0,1:T(8,128)}, f32[512,32]{0,1:T(8,128)S(1)}, u32[]{:S(2)}) copy-start(f32[512,32]{0,1:T(8,128)S(1)} %get-tuple-element.113) | copy-start | bytes 196612
  58.3 131.2 %copy-start.21 = (f32[512,32]{0,1:T(8,128)}, f32[512,32]{0,1:T(8,128)S(1)}, u32[]{:S(2)}) copy-start(f32[512,32]{0,1:T(8,128)S(1)} %get-tuple-element.114) | copy-start | bytes 196612
  70.1 58.1 %copy-start.2 = (bf16[512,1024]{1,0:T(8,128)(2,1)S(1)}, bf16[512,1024]{1,0:T(8,128)(2,1)}, u32[]{:S(2)}) copy-start(bf16[512,1024]{1,0:T(8,128)(2,1)} %param.22) | copy-start | bytes 3145732
  74.2 131.8 %copy-start.5 = (bf16[512,1024]{0,1:T(8,128)(2,1)}, bf16[512,1024]{0,1:T(8,128)(2,1)S(1)}, u32[]{:S(2)}) copy-start(bf16[512,1024]{0,1:T(8,128)(2,1)S(1)} %copy.48) | copy-start | bytes 3145732
  186.3 3.2 copy-start.7
  190.2 7.4 copy-start.8
  190.2 7.4 copy-start.10
  190.2 7.4 copy-start.12
  190.2 7.4 copy-start.14
  248.9 165.7 %all-gather.19.cloned.1.call-start = ((), (), s32[]{:S(2)}) async-start(), calls=%async_computation.14 | async-start | bytes 1622016 | tf_op jit(solution)/shard_map/all_gather | solution.py:122
  249.6 192.2 %all-gather.23.cloned.1.call-start = ((), (), s32[]{:S(2)}) async-start(), calls=%async_computation.16 | async-start | bytes 1622016 | tf_op jit(solution)/shard_map/all_gather | solution.py:124
  249.7 28.2 %collective-permute-start = (bf16[512,1024]{1,0:T(8,128)(2,1)}, bf16[512,1024]{1,0:T(8,128)(2,1)}, u32[]{:S(2)}, u32[]{:S(2)}) collective-permute-start(bf16[512,1024]{1,0:T(8,128)(2,1)} %param.24), channel_id=1, source_target_pairs={{0,8},{8,16},{16,24},{24,0},{1,9},{9,17},{17,25},{25,1},{2,10},{10... | collective-permute-start | bytes 3145736 | tf_op jit(solution)/shard_map/ppermute | solution.py:24
  250.3 93.5 %collective-permute-start.2 = (bf16[512,1024]{1,0:T(8,128)(2,1)}, bf16[512,1024]{1,0:T(8,128)(2,1)}, u32[]{:S(2)}, u32[]{:S(2)}) collective-permute-start(bf16[512,1024]{1,0:T(8,128)(2,1)} %param.24), channel_id=1, source_target_pairs={{8,0},{16,8},{24,16},{0,24},{9,1},{17,9},{25,17},{1,25},{10,2},{18... | collective-permute-start | bytes 3145736 | tf_op jit(solution)/shard_map/ppermute | solution.py:26
  277.9 81.9 %collective-permute-start.1 = (bf16[512,1024]{1,0:T(8,128)(2,1)}, bf16[512,1024]{1,0:T(8,128)(2,1)}, u32[]{:S(2)}, u32[]{:S(2)}) collective-permute-start(bf16[512,1024]{1,0:T(8,128)(2,1)} %collective-permute-done), channel_id=1, source_target_pairs={{0,8},{8,16},{16,24},{24,0},{1,9},{9,17},{17,25},{25,1},{2,10},{10... | collective-permute-start | bytes 3145736 | tf_op jit(solution)/shard_map/ppermute | solution.py:24
  277.9 329.9 %reduce-scatter.18.cloned.1.call-start = ((), (), s32[]{:S(2)}) async-start(), calls=%async_computation.18 | async-start | bytes 10485760 | tf_op jit(solution)/shard_map/reduce_scatter | solution.py:189
  441.8 11.8 copy-start.26
  453.6 3.5 copy-start.28
  453.6 3.5 copy-start.27
  453.6 3.5 copy-start.25
  463.2 224.3 %reduce-scatter.16.cloned.1.call-start = ((), (), s32[]{:S(2)}) async-start(), calls=%async_computation.17 | async-start | bytes 5242880 | tf_op jit(solution)/shard_map/reduce_scatter | solution.py:180
  470.9 275.2 %reduce-scatter.32.cloned.1.call-start = ((), (), s32[]{:S(2)}) async-start(), calls=%async_computation.25 | async-start | bytes 1769472
  480.9 291.3 %reduce-scatter.30.cloned.1.call-start = ((), (), s32[]{:S(2)}) async-start(), calls=%async_computation.24 | async-start | bytes 1769472
  490.8 323.4 %reduce-scatter.28.cloned.1.call-start = ((), (), s32[]{:S(2)}) async-start(), calls=%async_computation.23 | async-start | bytes 1769472
  501.0 457.2 %reduce-scatter.26.cloned.1.call-start = ((), (), s32[]{:S(2)}) async-start(), calls=%async_computation.22 | async-start | bytes 4325376 | tf_op jit(solution)/shard_map/reduce_scatter | solution.py:270
  687.5 4.6 copy-start.6
  697.0 400.7 %reduce-scatter.24.cloned.1.call-start = ((), (), s32[]{:S(2)}) async-start(), calls=%async_computation.21 | async-start | bytes 4325376 | tf_op jit(solution)/shard_map/reduce_scatter | solution.py:269
  701.2 7.8 copy-start.4
  709.0 1.3 copy-start
  713.9 523.7 %reduce-scatter.20.cloned.1.call-start = ((), (), s32[]{:S(2)}) async-start(), calls=%async_computation.19 | async-start | bytes 4325376 | tf_op jit(solution)/shard_map/reduce_scatter | solution.py:267
  722.6 8.4 copy-start.13
  731.1 3.8 copy-start.9
  731.1 3.8 copy-start.11
  734.9 1.6 copy-start.20
  734.9 1.6 copy-start.22
  737.2 1.6 copy-start.3
  737.3 5.2 copy-start.18
  742.2 635.1 %reduce-scatter.22.cloned.1.call-start = ((), (), s32[]{:S(2)}) async-start(), calls=%async_computation.20 | async-start | bytes 4325376 | tf_op jit(solution)/shard_map/reduce_scatter | solution.py:268
  746.1 70.0 %copy-start.1 = (f32[16,64,512]{2,1,0:T(8,128)S(1)}, f32[16,64,512]{2,1,0:T(8,128)}, u32[]{:S(2)}) copy-start(f32[16,64,512]{2,1,0:T(8,128)} %copy-done) | copy-start | bytes 6291460
  817.9 3.4 copy-start.17
  817.9 3.4 copy-start.24
  821.3 1.6 copy-start.15
  822.9 44.1 %copy-start.23 = (f32[512]{0:T(512)S(1)}, f32[512]{0:T(512)}, u32[]{:S(2)}) copy-start(f32[512]{0:T(512)} %get-tuple-element.115) | copy-start | bytes 6148
  (1 other events, 1.0 us)
Sparse Core Ops, SparseCore 0:
  10.9 59.1 all-gather.8
  72.9 55.2 all-gather.10
  131.1 55.2 all-gather.12
  189.0 55.2 all-gather.14
  246.0 24.1 all-gather.20
  272.2 116.6 all-gather.16
  390.8 23.7 all-gather.18
  416.5 25.2 all-gather.22
  463.3 144.4 reduce-scatter.17
  609.9 77.4 reduce-scatter.15
  691.1 38.9 reduce-scatter.31
  733.6 38.4 reduce-scatter.29
  775.8 38.4 reduce-scatter.27
  817.1 141.0 reduce-scatter.25
  961.0 136.6 reduce-scatter.23
  1100.5 137.0 reduce-scatter.19
  1240.4 136.8 reduce-scatter.21
